TPU v7x, 128 devices: a whole 4x4x4 slice. The times are simulated.
128 devices in a mesh: row: 32 (over y_lo, z, x), col: 4 (over y_hi, core).
Axes of the slice: x: 4, y: 4 (y_hi: 2, y_lo: 2; y = y_hi * 2 + y_lo), z: 4, core: 2. Of those that a mesh axis runs over, the one named last changes fastest.
Arguments:
- image: bfloat16 [18432, 1152], P(('row', 'col')), may hold values from -6 to 6
- text: bfloat16 [18432, 1152], P(('col', 'row')), may hold values from -6 to 6
- log_scale: float32 [], replicated, may hold values from 0.9 to 1.3
Outputs:
- loss_value: float32 [], replicated
- image_grad: float32 [18432, 1152], P(('row', 'col'))
- text_grad: float32 [18432, 1152], P(('col', 'row'))
All inputs are finite; a program needn't handle non-finite values.
Results may differ from a plain program's by a relative error of at most 0.00175.
Values may be sent and summed in bfloat16 or wider, within the bound.
No kernel may reach another device: no remote copies, remote signals or barrier semaphores. Data moves between devices by JAX's collectives and lax.ppermute only.
A program may use at most 128 MiB of HBM per device.

v0:
```python
import math

import jax
import jax.numpy as jnp
from jax import lax
from jax.experimental import pallas as pl
from jax.experimental.pallas import tpu as pltpu
from jax.sharding import Mesh, PartitionSpec as P

AXES = ("ylo", "z", "x", "yhi", "core")
RING = 4
TILE_SLOTS = 2
EXTRA = 16
UNITS = (256.0, 1.0, 2.0 ** -8, 2.0 ** -16, 2.0 ** -24)
VMEM_LIMIT = 12 * 1024 * 1024


def f32(*shape):
    return jax.ShapeDtypeStruct(shape, jnp.float32)


def bf16(*shape):
    return jax.ShapeDtypeStruct(shape, jnp.bfloat16)


def vmem_call(kernel, out_shape, name, flops, transcendentals, scalars, *args):
    vmem = pl.BlockSpec(memory_space=pltpu.VMEM)
    nbytes = sum(a.size * a.dtype.itemsize for a in args)
    nbytes += sum(math.prod(o.shape) * o.dtype.itemsize for o in out_shape)
    return pl.pallas_call(
        kernel,
        in_specs=[pl.BlockSpec(memory_space=pltpu.SMEM)] * len(scalars) + [vmem] * len(args),
        out_specs=[vmem] * len(out_shape),
        out_shape=out_shape,
        compiler_params=pltpu.CompilerParams(vmem_limit_bytes=VMEM_LIMIT),
        cost_estimate=pl.CostEstimate(flops=flops, bytes_accessed=nbytes, transcendentals=transcendentals),
        name=name,
    )(*scalars, *args)


def to_lanes(column):
    return jnp.broadcast_to(column, (column.shape[0], 128)).T[0:1, :]


def to_rows(line):
    return jnp.broadcast_to(line, (128, line.shape[1])).T[:, 0:1]


def merge(stats):
    top = stats[0][0]
    for stat in stats[1:]:
        top = jnp.maximum(top, stat[0])
    total = sum(stat[1] * jnp.exp2(stat[0] - top) for stat in stats)
    return [top, total] + [sum(stat[k] for stat in stats) for k in range(2, len(stats[0]))]


def place_refs(refs):
    return {axis: refs[k][0] for k, axis in enumerate(AXES)}


def image_block(place, h, slot):
    x = lax.rem(place["x"] + RING - slot % RING, RING)
    core = place["core"] if slot < RING else 1 - place["core"]
    yhi = place["yhi"] if h == 0 else 1 - place["yhi"]
    return ((place["ylo"] * 4 + place["z"]) * 4 + x) * 4 + yhi * 2 + core


def text_block(place, slot):
    z = lax.rem(place["z"] + RING - slot % RING, RING)
    ylo = place["ylo"] if slot < RING else 1 - place["ylo"]
    return (place["yhi"] * 2 + place["core"]) * 32 + (ylo * 4 + z) * 4 + place["x"]


def score_call(images, texts, scale, place, h, near_stats, rows, name):
    width = images[0].shape[1]
    sizes = [a.shape[0] for a in images]
    text_sizes = [a.shape[0] for a in texts]
    m, n = sum(sizes), sum(text_sizes)
    slots = m // rows
    before = near_stats[0].shape[1] if near_stats else 0
    keep_text = len(texts) > 1

    def kernel(scale_ref, *refs):
        place, refs = place_refs(refs), refs[len(AXES):]
        image_refs, refs = refs[:len(images)], refs[len(images):]
        text_refs, refs = refs[:len(texts)], refs[len(texts):]
        held, refs = refs[:len(near_stats)], refs[len(near_stats):]
        s_ref, x_ref, row_ref, col_ref = refs[:4]
        t_ref = refs[4] if keep_text else text_refs[0]

        def fill(target, sources, counts):
            at = 0
            for source, count in zip(sources, counts):
                target[pl.ds(at, count), :] = source[...]
                at += count

        if keep_text:
            fill(t_ref, text_refs, text_sizes)
        fill(x_ref, image_refs, sizes)
        tile = rows * TILE_SLOTS
        tiles = m // tile
        scale = scale_ref[0]
        col_parts = []

        def scores(i):
            s_ref[pl.ds(i * tile, tile), :] = scale * lax.dot_general(
                x_ref[pl.ds(i * tile, tile), :], t_ref[...], (((1,), (1,)), ((), ())),
                preferred_element_type=jnp.float32)

        def stats(i):
            s = s_ref[pl.ds(i * tile, tile), :]
            col_top = jnp.max(s, axis=0, keepdims=True)
            col_parts.append((col_top, jnp.sum(jnp.exp2(s - col_top), axis=0, keepdims=True)))
            for j in range(TILE_SLOTS):
                slot = i * TILE_SLOTS + j
                s = s_ref[pl.ds(slot * rows, rows), :]
                row_top = jnp.max(s, axis=1, keepdims=True)
                row_sum = jnp.sum(jnp.exp2(s - row_top), axis=1, keepdims=True)
                row_ref[0, pl.ds(before + slot, 1), :] = to_lanes(row_top)
                row_ref[1, pl.ds(before + slot, 1), :] = to_lanes(row_sum)

        scores(0)
        for i in range(tiles):
            if i + 1 < tiles:
                scores(i + 1)
            stats(i)
        top, total = merge(col_parts)
        for k in range(n // rows):
            at = slice(k * rows, (k + 1) * rows)
            part = [(top[:, at], total[:, at])]
            if held:
                part.append((held[1][0, pl.ds(k, 1), :], held[1][1, pl.ds(k, 1), :]))
            col_ref[0, pl.ds(k, 1), :], col_ref[1, pl.ds(k, 1), :] = merge(part)
        if held:
            row_ref[:, pl.ds(0, before), :] = held[0][...]
        row_ref[2, pl.ds(before, slots), :] = jnp.zeros((slots, rows), jnp.float32)
        for slot in range(slots):
            for k in range(n // rows):
                @pl.when(image_block(place, h, slot) == text_block(place, k))
                def _():
                    s = s_ref[pl.ds(slot * rows, rows), :][:, k * rows:(k + 1) * rows]
                    mask = (lax.broadcasted_iota(jnp.int32, (rows, 1), 0)
                            == lax.broadcasted_iota(jnp.int32, (1, rows), 1))
                    row_ref[2, pl.ds(before + slot, 1), :] = jnp.sum(jnp.where(mask, s, 0.0), axis=0, keepdims=True)

    out_shape = [f32(m, n), bf16(m, width), f32(3, before + slots, rows), f32(2, n // rows, rows)]
    out_shape += [bf16(n, width)] * keep_text
    return vmem_call(kernel, out_shape, name, 2 * m * n * width, 2 * m * n, [scale, *place],
                     *images, *texts, *near_stats)


def turned(ref, k, step):
    rings = []
    for lo in range(0, ref.shape[1], RING):
        rings.append(ref[k, pl.ds(lo + RING - step, step), :])
        rings.append(ref[k, pl.ds(lo, RING - step), :])
    return jnp.concatenate(rings, axis=0)


def swapped(ref, k, group):
    parts = []
    for lo in range(0, ref.shape[1], 2 * group):
        parts.append(ref[k, pl.ds(lo + group, group), :])
        parts.append(ref[k, pl.ds(lo, group), :])
    return jnp.concatenate(parts, axis=0)


def ring_merge_call(row, rows_in, col, cols_in):
    def kernel(*refs):
        row_refs, col_refs = refs[:RING], refs[RING:2 * RING]
        for own, out in ((row_refs, refs[-2]), (col_refs, refs[-1])):
            planes = out.shape[0]
            stats = [[own[0][k] for k in range(planes)]]
            for step in range(1, RING):
                stats.append([turned(own[step], k, step) for k in range(planes)])
            for k, value in enumerate(merge(stats)):
                out[k] = value

    return vmem_call(kernel, [f32(*row.shape), f32(*col.shape)], "merge_ring", 0, 0, [],
                     row, *rows_in, col, *cols_in)


def pair_merge_call(row, row_in, col, col_in, loss_scale):
    half = col.shape[1] // 2

    def kernel(row_ref, row_in_ref, col_ref, col_in_ref, row_out, lse_ref, loss_ref):
        planes = range(row_ref.shape[0])
        for k, value in enumerate(merge([
                [row_ref[k] for k in planes], [swapped(row_in_ref, k, row_ref.shape[1] // 2) for k in planes]])):
            row_out[k] = value
        top, total = merge([[col_ref[k] for k in range(2)], [swapped(col_in_ref, k, half) for k in range(2)]])
        lse = top + jnp.log2(total)
        lse_ref[...] = lse
        loss_ref[...] = jnp.sum(lse, axis=0, keepdims=True) * loss_scale

    return vmem_call(kernel, [f32(*row.shape), f32(*col.shape[1:]), f32(1, col.shape[2])], "merge_pair", 0, 0, [],
                     row, row_in, col, col_in)


def core_merge_call(row, row_in, loss_scale):
    def kernel(row_ref, row_in_ref, lse_ref, loss_ref):
        planes = range(row_ref.shape[0])
        top, total, own = merge([[row_ref[k] for k in planes], [swapped(row_in_ref, k, RING) for k in planes]])
        lse = top + jnp.log2(total)
        lse_ref[...] = lse
        loss_ref[...] = jnp.sum(lse - 2.0 * own, axis=0, keepdims=True) * loss_scale

    return vmem_call(kernel, [f32(*row.shape[1:]), f32(1, row.shape[2])], "merge_core", 0, 0, [], row, row_in)


def soft_weights(v, row_lse, col_lse, first_id, col_ids):
    ids = first_id + lax.broadcasted_iota(jnp.int32, (v.shape[0], 1), 0)
    soft = 0.5 * (jnp.exp2(v - to_rows(row_lse)) + jnp.exp2(v - col_lse))
    return (soft - jnp.where(ids == col_ids, 1.0, 0.0)).astype(jnp.bfloat16)


def weight_steps(w_ref, s_ref, row_ref, col_ref, place, h, rows):
    slots = range(col_ref.shape[0])
    col_lse = jnp.concatenate([col_ref[pl.ds(k, 1), :] for k in slots], axis=1)
    within = lax.broadcasted_iota(jnp.int32, (1, rows), 1)
    col_ids = jnp.concatenate([text_block(place, k) * rows + within for k in slots], axis=1)
    first = h * 2 * RING

    def weights(i):
        for j in range(TILE_SLOTS):
            slot = i * TILE_SLOTS + j
            at = pl.ds(slot * rows, rows)
            w_ref[at, :] = soft_weights(
                s_ref[at, :], row_ref[pl.ds(first + slot, 1), :], col_lse, image_block(place, h, slot) * rows, col_ids)

    return weights


def put_digits(part_ref, loss_ref, rows):
    left = jnp.sum(loss_ref[...], axis=1, keepdims=True)
    number = lax.broadcasted_iota(jnp.int32, (EXTRA, 1), 0)
    block = jnp.zeros((EXTRA, 1), jnp.float32)
    for k, unit in enumerate(UNITS):
        digit = jnp.floor(left * (1.0 / unit) + 0.5)
        left = left - digit * unit
        block = jnp.where(number == k, digit, block)
    for slot in range(part_ref.shape[0]):
        part_ref[slot, pl.ds(rows, EXTRA), :] = jnp.broadcast_to(block, (EXTRA, part_ref.shape[2]))


def put_slots(own_ref, other_ref, slot, part, rows):
    for j in range(part.shape[0] // rows):
        out = own_ref if slot + j < RING else other_ref
        out[(slot + j) % RING, pl.ds(0, rows), :] = part[j * rows:(j + 1) * rows]


def image_call(s, row_lse, col_lse, loss, place, text, rows, name):
    m, n = s.shape
    width = text.shape[1]

    def kernel(*refs):
        place, refs = place_refs(refs), refs[len(AXES):]
        s_ref, row_ref, col_ref, loss_ref, t_ref, w_ref, own_ref, other_ref = refs
        tile = rows * TILE_SLOTS
        tiles = m // tile
        weights = weight_steps(w_ref, s_ref, row_ref, col_ref, place, 1, rows)
        put_digits(own_ref, loss_ref, rows)
        other_ref[:, pl.ds(rows, EXTRA), :] = own_ref[:, pl.ds(rows, EXTRA), :]

        def dots(i):
            put_slots(own_ref, other_ref, i * TILE_SLOTS, jnp.dot(
                w_ref[pl.ds(i * tile, tile), :], t_ref[...], preferred_element_type=jnp.float32), rows)

        weights(0)
        for i in range(tiles):
            if i + 1 < tiles:
                weights(i + 1)
            dots(i)

    parts = [f32(RING, rows + EXTRA, width)] * 2
    return vmem_call(kernel, [bf16(m, n)] + parts, name, 2 * m * n * width, 2 * m * n,
                     place, s, row_lse, col_lse, loss, text)


def text_call(s, row_lse, col_lse, loss, place, x_near, w_far, x_far, rows, name):
    m, n = s.shape
    width = x_near.shape[1]
    chunk = 384

    def kernel(*refs):
        place, refs = place_refs(refs), refs[len(AXES):]
        s_ref, row_ref, col_ref, loss_ref, xn_ref, wf_ref, xf_ref, w_ref, part_ref = refs
        tiles = m // (rows * TILE_SLOTS)
        dims = (((0,), (0,)), ((), ()))
        weights = weight_steps(w_ref, s_ref, row_ref, col_ref, place, 0, rows)
        put_digits(part_ref, loss_ref, rows)
        weights(0)
        for j in range(width // chunk):
            at = pl.ds(j * chunk, chunk)
            part = lax.dot_general(wf_ref[...], xf_ref[:, at], dims, preferred_element_type=jnp.float32)
            for k in range(n // rows):
                part_ref[k, pl.ds(0, rows), at] = part[k * rows:(k + 1) * rows]
            if j + 1 < tiles:
                weights(j + 1)
        for j in range(width // chunk):
            at = pl.ds(j * chunk, chunk)
            part = lax.dot_general(w_ref[...], xn_ref[:, at], dims, preferred_element_type=jnp.float32)
            for k in range(n // rows):
                part_ref[k, pl.ds(0, rows), at] += part[k * rows:(k + 1) * rows]

    return vmem_call(kernel, [bf16(m, n), f32(n // rows, rows + EXTRA, width)], name,
                     4 * m * n * width, 2 * m * n, place, s, row_lse, col_lse, loss, x_near, w_far, x_far)


def near_call(w, text, loss, rows, name):
    m, n = w.shape
    width = text.shape[1]
    half = m // 2

    def kernel(w_ref, t_ref, loss_ref, own_ref, other_ref):
        put_digits(own_ref, loss_ref, rows)
        other_ref[:, pl.ds(rows, EXTRA), :] = own_ref[:, pl.ds(rows, EXTRA), :]
        for slot in (RING, 0):
            put_slots(own_ref, other_ref, slot, jnp.dot(
                w_ref[pl.ds(slot * rows, half), :], t_ref[...], preferred_element_type=jnp.float32), rows)

    parts = [f32(RING, rows + EXTRA, width)] * 2
    return vmem_call(kernel, parts, name, 2 * m * n * width, 0, [], w, text, loss)


def after(value, *others):
    return lax.optimization_barrier((value, *others))[0]


def ring_shift(value, axis, step):
    return lax.ppermute(value, axis, [(i, (i + step) % RING) for i in range(RING)])


def ring_split(value, axis, sign):
    pairs = []
    for i in range(RING):
        for core in range(2):
            target = (i + (sign if core == 0 else -sign)) % RING
            pairs.append((i * 2 + core, target * 2 + core))
    return lax.ppermute(value, (axis, "core"), pairs)


def swap(value, axis):
    return lax.ppermute(value, axis, [(0, 1), (1, 0)])


def ring_gather(value, axis, core):
    one = ring_shift(value, axis, 1)
    three = ring_shift(value, axis, 3)
    two = ring_split(jnp.where(core == 0, one, three), axis, 1)
    return [value, one, two, three]


def summed(own, other):
    return own + other.astype(jnp.float32)


def ring_outgoing(one, three, through, core):
    through = through.astype(jnp.float32)
    left = one + jnp.where(core == 0, through, 0.0)
    right = three + jnp.where(core == 0, 0.0, through)
    return left.astype(jnp.float16), right.astype(jnp.float16)


def ring_arrived(own, left, right, axis):
    return own + ring_shift(left, axis, -1).astype(jnp.float32) + ring_shift(right, axis, 1).astype(jnp.float32)


def on_device(image, text, log_scale):
    inverse_temp = jnp.exp(log_scale)
    rows = image.shape[0]
    core = lax.axis_index("core")
    place = [lax.axis_index(axis).reshape(1) for axis in AXES]

    text_far = swap(text, "ylo")
    image = after(image, text_far)
    image_far = swap(image, "yhi")
    text_near_slots = ring_gather(text, "z", core)
    text_far_slots = ring_gather(text_far, "z", core)
    image_near_slots = ring_gather(image, "x", core)
    image_far_slots = ring_gather(image_far, "x", core)
    image_near_other = swap(jnp.concatenate(image_near_slots), "core")
    image_far_other = [swap(a, "core") for a in image_far_slots]

    scale = (inverse_temp * jnp.float32(math.log2(math.e))).reshape(1)
    s_near, x_near, row_stat, col_stat, t_all = score_call(
        image_near_slots + [image_near_other], text_near_slots + text_far_slots, scale, place, 0, [], rows,
        "score_near")
    s_far, x_far, row_stat, col_stat = score_call(
        image_far_slots + image_far_other, [t_all], scale, place, 1, [row_stat, col_stat], rows, "score_far")

    loss_scale = math.log(2.0) / (2 * 128 * rows)
    row_stat, col_stat = ring_merge_call(
        row_stat, [ring_shift(row_stat, "x", step) for step in (1, 2, 3)],
        col_stat, [ring_shift(col_stat, "z", step) for step in (1, 2, 3)])
    row_stat, col_lse, col_loss = pair_merge_call(
        row_stat, swap(row_stat, "yhi"), col_stat, swap(col_stat, "ylo"), loss_scale)
    row_lse, row_loss = core_merge_call(row_stat, swap(row_stat, "core"), loss_scale)

    w_far, far_own, far_part = image_call(s_far, row_lse, col_lse, col_loss, place, t_all, rows, "image_far")
    far_send = far_part.astype(jnp.float16)
    far_other = swap(far_send, "core")
    w_near, text_part = text_call(
        s_near, after(row_lse, far_send), col_lse, row_loss, place, x_near, w_far, x_far, rows, "text_all")
    near_text, far_text = text_part[:RING], text_part[RING:]
    text_two = jnp.stack([near_text[2], far_text[2]]).astype(jnp.float16)
    text_through = ring_split(text_two, "z", -1)
    far_two = summed(far_own[2], after(far_other, text_two)[2]).astype(jnp.float16)
    far_through = ring_split(far_two, "x", -1)
    near_own, near_part = near_call(after(w_near, far_two), t_all, col_loss, rows, "image_near")
    near_send = near_part.astype(jnp.float16)
    near_other = swap(near_send, "core")

    far_left, far_right = ring_outgoing(
        summed(far_own[1], far_other[1]), summed(far_own[3], far_other[3]), after(far_through, near_send), core)
    far_text_left, far_text_right = ring_outgoing(
        far_text[1], far_text[3], after(text_through, far_left)[1], core)
    near_two = summed(near_own[2], after(near_other, far_text_left)[2]).astype(jnp.float16)
    near_through = ring_split(near_two, "x", -1)
    near_text_left, near_text_right = ring_outgoing(
        near_text[1], near_text[3], after(text_through, near_two)[0], core)
    image_far_sum = ring_arrived(
        summed(far_own[0], after(far_other, near_text_left)[0]), far_left, far_right, "x").astype(jnp.float16)
    text_far_sum = ring_arrived(
        after(far_text[0], image_far_sum), far_text_left, far_text_right, "z").astype(jnp.float16)
    near_left, near_right = ring_outgoing(
        summed(near_own[1], near_other[1]), summed(near_own[3], near_other[3]), after(near_through, text_far_sum), core)
    text_sum = (ring_arrived(after(near_text[0], near_left), near_text_left, near_text_right, "z")
                + swap(text_far_sum, "ylo").astype(jnp.float32))
    image_sum = (ring_arrived(summed(near_own[0], near_other[0]), near_left, near_right, "x")
                 + swap(image_far_sum, "yhi").astype(jnp.float32))

    digits = text_sum[rows:, 0] + image_sum[rows:, 0]
    loss_value = sum(digits[k] * unit for k, unit in enumerate(UNITS))
    return loss_value, inverse_temp * image_sum[:rows], inverse_temp * text_sum[:rows]


def solution(mesh):
    fine = Mesh(mesh.devices.reshape(2, 4, 4, 2, 2), AXES)
    text_spec = P(("yhi", "core", "ylo", "z", "x"), None)
    return jax.shard_map(
        on_device, mesh=fine, in_specs=(P(AXES, None), text_spec, P()),
        out_specs=(P(), P(AXES, None), text_spec), check_vma=False
    )
```

profile of v0, /device:TPU:0, one launch (start us, length us, event | category | flops | bytes accessed | tf_op | source)
XLA Modules:
  0.0 176.4 jit_solution(7325897667196377726)
XLA Ops:
  2.4 8.1 %collective-permute-done.refs_14_ = bf16[144,1152]{1,0:T(8,128)(2,1)} collective-permute-done((bf16[144,1152]{1,0:T(8,128)(2,1)}, bf16[144,1152]{1,0:T(8,128)(2,1)}, u32[]{:S(2)}, u32[]{:S(2)}) %collective-permute-start) | collective-permute-done | bytes 331808 | tf_op jit(solution)/shard_map/ppermute | solution.py:344
  10.5 2.9 %collective-permute-start.2 = (bf16[144,1152]{1,0:T(8,128)(2,1)}, bf16[144,1152]{1,0:T(8,128)(2,1)S(1)}, u32[]{:S(2)}, u32[]{:S(2)}) collective-permute-start(bf16[144,1152]{1,0:T(8,128)(2,1)} %refs_5_), channel_id=1, source_target_pairs={{0,12},{4,0},{8,4},{12,8},{1,13},{5,1},{9,5},{13,9},{2,14},{6,2},{... | collective-permute-start | bytes 995336 | tf_op jit(solution)/shard_map/ppermute | solution.py:331
  17.4 3.2 %collective-permute-start.11 = (bf16[144,1152]{1,0:T(8,128)(2,1)}, bf16[144,1152]{1,0:T(8,128)(2,1)}, u32[]{:S(2)}, u32[]{:S(2)}) collective-permute-start(bf16[144,1152]{1,0:T(8,128)(2,1)} %refs_5_), channel_id=1, source_target_pairs={{0,2},{2,0},{1,3},{3,1},{4,6},{6,4},{5,7},{7,5},{8,10},{10,8},{9,1... | collective-permute-start | bytes 995336 | tf_op jit(solution)/shard_map/ppermute | solution.py:344
  20.6 3.3 %collective-permute-start.9 = (bf16[144,1152]{1,0:T(8,128)(2,1)}, bf16[144,1152]{1,0:T(8,128)(2,1)S(1)}, u32[]{:S(2)}, u32[]{:S(2)}) collective-permute-start(bf16[144,1152]{1,0:T(8,128)(2,1)} %collective-permute-done.refs_14_), channel_id=1, source_target_pairs={{0,48},{16,0},{32,16},{48,32},{1,49},{17,1},{33,17},{49,33},{2,50}... | collective-permute-start | bytes 995336 | tf_op jit(solution)/shard_map/ppermute | solution.py:331
  26.1 2.2 %collective-permute-start.7 = (bf16[144,1152]{1,0:T(8,128)(2,1)S(1)}, bf16[144,1152]{1,0:T(8,128)(2,1)S(1)}, u32[]{:S(2)}, u32[]{:S(2)}) collective-permute-start(bf16[144,1152]{1,0:T(8,128)(2,1)S(1)} %broadcast_select_fusion.2), channel_id=1, source_target_pairs={{0,16},{1,49},{16,32},{17,1},{32,48},{33,17},{48,0},{49,33},{2,18}... | collective-permute-start | bytes 995336 | tf_op jit(solution)/shard_map/ppermute | solution.py:340
  28.3 2.3 %collective-permute-start.13 = (bf16[144,1152]{1,0:T(8,128)(2,1)}, bf16[144,1152]{1,0:T(8,128)(2,1)S(1)}, u32[]{:S(2)}, u32[]{:S(2)}) collective-permute-start(bf16[144,1152]{1,0:T(8,128)(2,1)} %collective-permute-done.11.refs_5_), channel_id=1, source_target_pairs={{0,12},{4,0},{8,4},{12,8},{1,13},{5,1},{9,5},{13,9},{2,14},{6,2},{... | collective-permute-start | bytes 995336 | tf_op jit(solution)/shard_map/ppermute | solution.py:331
  30.7 2.9 %collective-permute-done.3.refs_7_ = bf16[144,1152]{1,0:T(8,128)(2,1)S(1)} collective-permute-done((bf16[144,1152]{1,0:T(8,128)(2,1)S(1)}, bf16[144,1152]{1,0:T(8,128)(2,1)S(1)}, u32[]{:S(2)}, u32[]{:S(2)}) %collective-permute-start.3) | collective-permute-done | bytes 331808 | tf_op jit(solution)/shard_map/ppermute | solution.py:340
  35.8 2.4 %collective-permute-start.10 = (bf16[144,1152]{1,0:T(8,128)(2,1)S(1)}, bf16[144,1152]{1,0:T(8,128)(2,1)S(1)}, u32[]{:S(2)}, u32[]{:S(2)}) collective-permute-start(bf16[144,1152]{1,0:T(8,128)(2,1)S(1)} %broadcast_select_fusion.1), channel_id=1, source_target_pairs={{0,16},{1,49},{16,32},{17,1},{32,48},{33,17},{48,0},{49,33},{2,18}... | collective-permute-start | bytes 995336 | tf_op jit(solution)/shard_map/ppermute | solution.py:340
  38.2 3.9 %collective-permute-done.12.refs_6_ = bf16[144,1152]{1,0:T(8,128)(2,1)S(1)} collective-permute-done((bf16[144,1152]{1,0:T(8,128)(2,1)}, bf16[144,1152]{1,0:T(8,128)(2,1)S(1)}, u32[]{:S(2)}, u32[]{:S(2)}) %collective-permute-start.12) | collective-permute-done | bytes 331808 | tf_op jit(solution)/shard_map/ppermute | solution.py:331
  44.9 5.7 %collective-permute-done.14.refs_7_ = bf16[144,1152]{1,0:T(8,128)(2,1)} collective-permute-done((bf16[144,1152]{1,0:T(8,128)(2,1)S(1)}, bf16[144,1152]{1,0:T(8,128)(2,1)}, u32[]{:S(2)}, u32[]{:S(2)}) %collective-permute-start.14) | collective-permute-done | bytes 331808 | tf_op jit(solution)/shard_map/ppermute | solution.py:340
  54.3 19.8 %score_near.1 = (f32[1152,1152]{1,0:T(8,128)S(1)}, bf16[1152,1152]{1,0:T(8,128)(2,1)S(1)}, f32[3,8,144]{2,1,0:T(8,128)S(1)}, f32[2,8,144]{2,1,0:T(8,128)S(1)}, bf16[1152,1152]{1,0:T(8,128)(2,1)S(1)}) custom-call(f32[1]{0:T(128)} %bitcast.5.scale_ref, s32[1]{0:T(128)} %bitcast.refs_0_, s32[1]{0:T(128)} %bitcast.1.refs_1_, s32[1]{0:T(128)} %bitcast.2.refs_2_, ...), custom_call_target="tpu_custom_call" | custom-call | flops 3057647616 | bytes 15948288 | tf_op jit(solution)/shard_map/score_near/pallas_call | solution.py:30
  74.1 6.8 %score_far.1 = (f32[1152,1152]{1,0:T(8,128)S(1)}, bf16[1152,1152]{1,0:T(8,128)(2,1)S(1)}, f32[3,16,144]{2,1,0:T(8,128)S(1)}, f32[2,8,144]{2,1,0:T(8,128)S(1)}) custom-call(f32[1]{0:T(128)} %bitcast.5.scale_ref, s32[1]{0:T(128)} %bitcast.refs_0_, s32[1]{0:T(128)} %bitcast.1.refs_1_, s32[1]{0:T(128)} %bitcast.2.refs_2_, s32[1]{0:T(128)} %bitcast.3.refs_3_, ...), custom_call_target="tpu_custom_call" | custom-call | flops 3057647616 | bytes 13330944 | tf_op jit(solution)/shard_map/score_far/pallas_call | solution.py:30
  85.1 2.4 %collective-permute-start.23 = (f32[2,8,144]{2,1,0:T(8,128)S(1)}, f32[2,8,144]{2,1,0:T(8,128)S(1)}, u32[]{:S(2)}, u32[]{:S(2)}) collective-permute-start(f32[2,8,144]{2,1,0:T(8,128)S(1)} %get-tuple-element.44.refs_4_), channel_id=1, source_target_pairs={{0,32},{16,48},{32,0},{48,16},{1,33},{17,49},{33,1},{49,17},{2,34}... | collective-permute-start | bytes 27656 | tf_op jit(solution)/shard_map/ppermute | solution.py:331
  92.5 3.0 %collective-permute-start.25 = (f32[3,16,144]{2,1,0:T(8,128)S(1)}, f32[3,16,144]{2,1,0:T(8,128)S(1)}, u32[]{:S(2)}, u32[]{:S(2)}) collective-permute-start(f32[3,16,144]{2,1,0:T(8,128)S(1)} %get-tuple-element.45.row_ref), channel_id=1, source_target_pairs={{0,2},{2,0},{1,3},{3,1},{4,6},{6,4},{5,7},{7,5},{8,10},{10,8},{9,1... | collective-permute-start | bytes 82952 | tf_op jit(solution)/shard_map/ppermute | solution.py:344
  96.4 2.8 %collective-permute-done.26.col_in_ref = f32[2,8,144]{2,1,0:T(8,128)S(1)} collective-permute-done((f32[2,8,144]{2,1,0:T(8,128)S(1)}, f32[2,8,144]{2,1,0:T(8,128)S(1)}, u32[]{:S(2)}, u32[]{:S(2)}) %collective-permute-start.26) | collective-permute-done | bytes 9248 | tf_op jit(solution)/shard_map/ppermute | solution.py:344
  100.6 5.2 %image_far.1 = (bf16[1152,1152]{1,0:T(8,128)(2,1)S(1)}, f32[4,160,1152]{2,1,0:T(8,128)S(1)}, f32[4,160,1152]{2,1,0:T(8,128)S(1)}) custom-call(s32[1]{0:T(128)} %bitcast.refs_0_, s32[1]{0:T(128)} %bitcast.1.refs_1_, s32[1]{0:T(128)} %bitcast.2.refs_2_, s32[1]{0:T(128)} %bitcast.3.refs_3_, s32[1]{0:T(128)} %bitcast.4.refs_4_, ...), custom_call_target="tpu_custom_call" | custom-call | flops 3057647616 | bytes 16529472 | tf_op jit(solution)/shard_map/image_far/pallas_call | solution.py:30
  106.6 10.7 %text_all.1 = (bf16[1152,1152]{1,0:T(8,128)(2,1)S(1)}, f32[8,160,1152]{2,1,0:T(8,128)S(1)}) custom-call(s32[1]{0:T(128)} %bitcast.refs_0_, s32[1]{0:T(128)} %bitcast.1.refs_1_, s32[1]{0:T(128)} %bitcast.2.refs_2_, s32[1]{0:T(128)} %bitcast.3.refs_3_, s32[1]{0:T(128)} %bitcast.4.refs_4_, f32[1152,1152]{1,0:T(8,128)S(1)} %get-tuple-element.39.refs_5_, ...), custom_call_target="tpu_custom_call" | custom-call | flops 6115295232 | bytes 21837888 | tf_op jit(solution)/shard_map/text_all/pallas_call | solution.py:30
  118.1 4.1 %image_near.1 = (f32[4,160,1152]{2,1,0:T(8,128)S(1)}, f32[4,160,1152]{2,1,0:T(8,128)S(1)}) custom-call(bf16[1152,1152]{1,0:T(8,128)(2,1)S(1)} %get-tuple-element.62.w_ref, bf16[1152,1152]{1,0:T(8,128)(2,1)S(1)} %get-tuple-element.40.refs_13_.refs_9_.t_ref, f32[1,144]{1,0:T(1,128)S(1)} %get-tuple-element.51.refs_8_.loss_ref), custom_call_target="tpu_custom_call" | custom-call | flops 3057647616 | bytes 11207232 | tf_op jit(solution)/shard_map/image_near/pallas_call | solution.py:30
  122.8 2.7 %collective-permute-start.31 = (f16[160,1152]{1,0:T(8,128)(2,1)S(1)}, f16[160,1152]{1,0:T(8,128)(2,1)S(1)}, u32[]{:S(2)}, u32[]{:S(2)}) collective-permute-start(f16[160,1152]{1,0:T(8,128)(2,1)S(1)} %fusion.20), channel_id=1, source_target_pairs={{0,12},{1,5},{4,0},{5,9},{8,4},{9,13},{12,8},{13,1},{2,14},{3,7},{... | collective-permute-start | bytes 1105928 | tf_op jit(solution)/shard_map/ppermute | solution.py:340
  127.2 3.4 %collective-permute-done.31 = f16[160,1152]{1,0:T(8,128)(2,1)S(1)} collective-permute-done((f16[160,1152]{1,0:T(8,128)(2,1)S(1)}, f16[160,1152]{1,0:T(8,128)(2,1)S(1)}, u32[]{:S(2)}, u32[]{:S(2)}) %collective-permute-start.31) | collective-permute-done | bytes 368672 | tf_op jit(solution)/shard_map/ppermute | solution.py:340
  134.7 2.3 %collective-permute-done.30 = f16[2,160,1152]{2,1,0:T(8,128)(2,1)S(1)} collective-permute-done((f16[2,160,1152]{2,1,0:T(8,128)(2,1)S(1)}, f16[2,160,1152]{2,1,0:T(8,128)(2,1)S(1)}, u32[]{:S(2)}, u32[]{:S(2)}) %collective-permute-start.30) | collective-permute-done | bytes 737312 | tf_op jit(solution)/shard_map/ppermute | solution.py:340
  137.7 2.8 %collective-permute-start.35 = (f16[160,1152]{1,0:T(8,128)(2,1)S(1)}, f16[160,1152]{1,0:T(8,128)(2,1)S(1)}, u32[]{:S(2)}, u32[]{:S(2)}) collective-permute-start(f16[160,1152]{1,0:T(8,128)(2,1)S(1)} %get-tuple-element.76), channel_id=1, source_target_pairs={{0,48},{16,0},{32,16},{48,32},{1,49},{17,1},{33,17},{49,33},{2,50}... | collective-permute-start | bytes 1105928 | tf_op jit(solution)/shard_map/ppermute | solution.py:331
  154.3 6.6 %collective-permute-done.39 = f16[160,1152]{1,0:T(8,128)(2,1)S(1)} collective-permute-done((f16[160,1152]{1,0:T(8,128)(2,1)S(1)}, f16[160,1152]{1,0:T(8,128)(2,1)S(1)}, u32[]{:S(2)}, u32[]{:S(2)}) %collective-permute-start.39) | collective-permute-done | bytes 368672 | tf_op jit(solution)/shard_map/ppermute | solution.py:344
  163.2 6.9 %collective-permute-done.41 = f16[160,1152]{1,0:T(8,128)(2,1)S(1)} collective-permute-done((f16[160,1152]{1,0:T(8,128)(2,1)S(1)}, f16[160,1152]{1,0:T(8,128)(2,1)S(1)}, u32[]{:S(2)}, u32[]{:S(2)}) %collective-permute-start.41) | collective-permute-done | bytes 368672 | tf_op jit(solution)/shard_map/ppermute | solution.py:331
  (106 shorter events, 53.9 us)
Async XLA Ops:
  13.4 11.8 %collective-permute-start.5 = (bf16[144,1152]{1,0:T(8,128)(2,1)}, bf16[144,1152]{1,0:T(8,128)(2,1)S(1)}, u32[]{:S(2)}, u32[]{:S(2)}) collective-permute-start(bf16[144,1152]{1,0:T(8,128)(2,1)} %refs_10_.1), channel_id=1, source_target_pairs={{0,16},{16,32},{32,48},{48,0},{1,17},{17,33},{33,49},{49,1},{2,18}... | collective-permute-start | bytes 995336 | tf_op jit(solution)/shard_map/ppermute | solution.py:331
  15.3 10.7 %collective-permute-start.6 = (bf16[144,1152]{1,0:T(8,128)(2,1)}, bf16[144,1152]{1,0:T(8,128)(2,1)S(1)}, u32[]{:S(2)}, u32[]{:S(2)}) collective-permute-start(bf16[144,1152]{1,0:T(8,128)(2,1)} %refs_10_.1), channel_id=1, source_target_pairs={{0,48},{16,0},{32,16},{48,32},{1,49},{17,1},{33,17},{49,33},{2,50}... | collective-permute-start | bytes 995336 | tf_op jit(solution)/shard_map/ppermute | solution.py:331
  17.4 10.9 %collective-permute-start.11 = (bf16[144,1152]{1,0:T(8,128)(2,1)}, bf16[144,1152]{1,0:T(8,128)(2,1)}, u32[]{:S(2)}, u32[]{:S(2)}) collective-permute-start(bf16[144,1152]{1,0:T(8,128)(2,1)} %refs_5_), channel_id=1, source_target_pairs={{0,2},{2,0},{1,3},{3,1},{4,6},{6,4},{5,7},{7,5},{8,10},{10,8},{9,1... | collective-permute-start | bytes 995336 | tf_op jit(solution)/shard_map/ppermute | solution.py:344
  20.6 15.1 %collective-permute-start.9 = (bf16[144,1152]{1,0:T(8,128)(2,1)}, bf16[144,1152]{1,0:T(8,128)(2,1)S(1)}, u32[]{:S(2)}, u32[]{:S(2)}) collective-permute-start(bf16[144,1152]{1,0:T(8,128)(2,1)} %collective-permute-done.refs_14_), channel_id=1, source_target_pairs={{0,48},{16,0},{32,16},{48,32},{1,49},{17,1},{33,17},{49,33},{2,50}... | collective-permute-start | bytes 995336 | tf_op jit(solution)/shard_map/ppermute | solution.py:331
  23.9 11.8 %collective-permute-start.8 = (bf16[144,1152]{1,0:T(8,128)(2,1)}, bf16[144,1152]{1,0:T(8,128)(2,1)S(1)}, u32[]{:S(2)}, u32[]{:S(2)}) collective-permute-start(bf16[144,1152]{1,0:T(8,128)(2,1)} %collective-permute-done.refs_14_), channel_id=1, source_target_pairs={{0,16},{16,32},{32,48},{48,0},{1,17},{17,33},{33,49},{49,1},{2,18}... | collective-permute-start | bytes 995336 | tf_op jit(solution)/shard_map/ppermute | solution.py:331
  26.1 16.2 %collective-permute-start.7 = (bf16[144,1152]{1,0:T(8,128)(2,1)S(1)}, bf16[144,1152]{1,0:T(8,128)(2,1)S(1)}, u32[]{:S(2)}, u32[]{:S(2)}) collective-permute-start(bf16[144,1152]{1,0:T(8,128)(2,1)S(1)} %broadcast_select_fusion.2), channel_id=1, source_target_pairs={{0,16},{1,49},{16,32},{17,1},{32,48},{33,17},{48,0},{49,33},{2,18}... | collective-permute-start | bytes 995336 | tf_op jit(solution)/shard_map/ppermute | solution.py:340
  35.8 15.6 %collective-permute-start.4 = (bf16[576,1152]{1,0:T(8,128)(2,1)}, bf16[576,1152]{1,0:T(8,128)(2,1)}, u32[]{:S(2)}, u32[]{:S(2)}) collective-permute-start(bf16[576,1152]{1,0:T(8,128)(2,1)} %pad_maximum_fusion), channel_id=1, source_target_pairs={{0,1},{1,0},{2,3},{3,2},{4,5},{5,4},{6,7},{7,6},{8,9},{9,8},{10,11... | collective-permute-start | bytes 3981320 | tf_op jit(solution)/shard_map/ppermute | solution.py:344
  42.3 31.8 %collective-permute-start.15 = (bf16[144,1152]{1,0:T(8,128)(2,1)}, bf16[144,1152]{1,0:T(8,128)(2,1)}, u32[]{:S(2)}, u32[]{:S(2)}) collective-permute-start(bf16[144,1152]{1,0:T(8,128)(2,1)} %collective-permute-done.11.refs_5_), channel_id=1, source_target_pairs={{0,1},{1,0},{2,3},{3,2},{4,5},{5,4},{6,7},{7,6},{8,9},{9,8},{10,11... | collective-permute-start | bytes 995336 | tf_op jit(solution)/shard_map/ppermute | solution.py:344
  43.1 31.0 %collective-permute-start.18 = (bf16[144,1152]{1,0:T(8,128)(2,1)S(1)}, bf16[144,1152]{1,0:T(8,128)(2,1)}, u32[]{:S(2)}, u32[]{:S(2)}) collective-permute-start(bf16[144,1152]{1,0:T(8,128)(2,1)S(1)} %collective-permute-done.13.refs_8_), channel_id=1, source_target_pairs={{0,1},{1,0},{2,3},{3,2},{4,5},{5,4},{6,7},{7,6},{8,9},{9,8},{10,11... | collective-permute-start | bytes 995336 | tf_op jit(solution)/shard_map/ppermute | solution.py:344
  44.9 29.2 %collective-permute-start.16 = (bf16[144,1152]{1,0:T(8,128)(2,1)S(1)}, bf16[144,1152]{1,0:T(8,128)(2,1)}, u32[]{:S(2)}, u32[]{:S(2)}) collective-permute-start(bf16[144,1152]{1,0:T(8,128)(2,1)S(1)} %collective-permute-done.12.refs_6_), channel_id=1, source_target_pairs={{0,1},{1,0},{2,3},{3,2},{4,5},{5,4},{6,7},{7,6},{8,9},{9,8},{10,11... | collective-permute-start | bytes 995336 | tf_op jit(solution)/shard_map/ppermute | solution.py:344
  50.7 23.4 %collective-permute-start.17 = (bf16[144,1152]{1,0:T(8,128)(2,1)}, bf16[144,1152]{1,0:T(8,128)(2,1)}, u32[]{:S(2)}, u32[]{:S(2)}) collective-permute-start(bf16[144,1152]{1,0:T(8,128)(2,1)} %collective-permute-done.14.refs_7_), channel_id=1, source_target_pairs={{0,1},{1,0},{2,3},{3,2},{4,5},{5,4},{6,7},{7,6},{8,9},{9,8},{10,11... | collective-permute-start | bytes 995336 | tf_op jit(solution)/shard_map/ppermute | solution.py:344
  80.9 11.5 %collective-permute-start.21 = (f32[3,16,144]{2,1,0:T(8,128)S(1)}, f32[3,16,144]{2,1,0:T(8,128)S(1)}, u32[]{:S(2)}, u32[]{:S(2)}) collective-permute-start(f32[3,16,144]{2,1,0:T(8,128)S(1)} %get-tuple-element.43.refs_0_), channel_id=1, source_target_pairs={{0,12},{4,0},{8,4},{12,8},{1,13},{5,1},{9,5},{13,9},{2,14},{6,2},{... | collective-permute-start | bytes 82952 | tf_op jit(solution)/shard_map/ppermute | solution.py:331
  81.0 11.4 %collective-permute-start.20 = (f32[3,16,144]{2,1,0:T(8,128)S(1)}, f32[3,16,144]{2,1,0:T(8,128)S(1)}, u32[]{:S(2)}, u32[]{:S(2)}) collective-permute-start(f32[3,16,144]{2,1,0:T(8,128)S(1)} %get-tuple-element.43.refs_0_), channel_id=1, source_target_pairs={{0,8},{4,12},{8,0},{12,4},{1,9},{5,13},{9,1},{13,5},{2,10},{6,14},... | collective-permute-start | bytes 82952 | tf_op jit(solution)/shard_map/ppermute | solution.py:331
  106.0 12.1 %collective-permute-start.28 = (f16[4,160,1152]{2,1,0:T(8,128)(2,1)S(1)}, f16[4,160,1152]{2,1,0:T(8,128)(2,1)S(1)}, u32[]{:S(2)}, u32[]{:S(2)}) collective-permute-start(f16[4,160,1152]{2,1,0:T(8,128)(2,1)S(1)} %convert_element_type.137), channel_id=1, source_target_pairs={{0,1},{1,0},{2,3},{3,2},{4,5},{5,4},{6,7},{7,6},{8,9},{9,8},{10,11... | collective-permute-start | bytes 4423688 | tf_op jit(solution)/shard_map/ppermute | solution.py:344
  122.4 18.1 %collective-permute-start.29 = (f16[4,160,1152]{2,1,0:T(8,128)(2,1)S(1)}, f16[4,160,1152]{2,1,0:T(8,128)(2,1)S(1)}, u32[]{:S(2)}, u32[]{:S(2)}) collective-permute-start(f16[4,160,1152]{2,1,0:T(8,128)(2,1)S(1)} %convert_element_type.141), channel_id=1, source_target_pairs={{0,1},{1,0},{2,3},{3,2},{4,5},{5,4},{6,7},{7,6},{8,9},{9,8},{10,11... | collective-permute-start | bytes 4423688 | tf_op jit(solution)/shard_map/ppermute | solution.py:344
  125.5 11.5 %collective-permute-start.30 = (f16[2,160,1152]{2,1,0:T(8,128)(2,1)S(1)}, f16[2,160,1152]{2,1,0:T(8,128)(2,1)S(1)}, u32[]{:S(2)}, u32[]{:S(2)}) collective-permute-start(f16[2,160,1152]{2,1,0:T(8,128)(2,1)S(1)} %pad_maximum_fusion.1), channel_id=1, source_target_pairs={{0,48},{1,17},{16,0},{17,33},{32,16},{33,49},{48,32},{49,1},{2,50}... | collective-permute-start | bytes 2211848 | tf_op jit(solution)/shard_map/ppermute | solution.py:340
  130.9 11.8 %collective-permute-start.34 = (f16[160,1152]{1,0:T(8,128)(2,1)S(1)}, f16[160,1152]{1,0:T(8,128)(2,1)S(1)}, u32[]{:S(2)}, u32[]{:S(2)}) collective-permute-start(f16[160,1152]{1,0:T(8,128)(2,1)S(1)} %get-tuple-element.82), channel_id=1, source_target_pairs={{0,4},{4,8},{8,12},{12,0},{1,5},{5,9},{9,13},{13,1},{2,6},{6,10},{... | collective-permute-start | bytes 1105928 | tf_op jit(solution)/shard_map/ppermute | solution.py:331
  132.8 11.8 %collective-permute-start.33 = (f16[160,1152]{1,0:T(8,128)(2,1)S(1)}, f16[160,1152]{1,0:T(8,128)(2,1)S(1)}, u32[]{:S(2)}, u32[]{:S(2)}) collective-permute-start(f16[160,1152]{1,0:T(8,128)(2,1)S(1)} %get-tuple-element.81), channel_id=1, source_target_pairs={{0,12},{4,0},{8,4},{12,8},{1,13},{5,1},{9,5},{13,9},{2,14},{6,2},{... | collective-permute-start | bytes 1105928 | tf_op jit(solution)/shard_map/ppermute | solution.py:331
  137.7 11.8 %collective-permute-start.35 = (f16[160,1152]{1,0:T(8,128)(2,1)S(1)}, f16[160,1152]{1,0:T(8,128)(2,1)S(1)}, u32[]{:S(2)}, u32[]{:S(2)}) collective-permute-start(f16[160,1152]{1,0:T(8,128)(2,1)S(1)} %get-tuple-element.76), channel_id=1, source_target_pairs={{0,48},{16,0},{32,16},{48,32},{1,49},{17,1},{33,17},{49,33},{2,50}... | collective-permute-start | bytes 1105928 | tf_op jit(solution)/shard_map/ppermute | solution.py:331
  140.8 21.4 %collective-permute-start.37 = (f16[160,1152]{1,0:T(8,128)(2,1)S(1)}, f16[160,1152]{1,0:T(8,128)(2,1)S(1)}, u32[]{:S(2)}, u32[]{:S(2)}) collective-permute-start(f16[160,1152]{1,0:T(8,128)(2,1)S(1)} %get-tuple-element.74), channel_id=1, source_target_pairs={{0,48},{16,0},{32,16},{48,32},{1,49},{17,1},{33,17},{49,33},{2,50}... | collective-permute-start | bytes 1105928 | tf_op jit(solution)/shard_map/ppermute | solution.py:331
  144.7 18.5 %collective-permute-start.42 = (f16[160,1152]{1,0:T(8,128)(2,1)S(1)}, f16[160,1152]{1,0:T(8,128)(2,1)S(1)}, u32[]{:S(2)}, u32[]{:S(2)}) collective-permute-start(f16[160,1152]{1,0:T(8,128)(2,1)S(1)} %fusion.19), channel_id=1, source_target_pairs={{0,2},{2,0},{1,3},{3,1},{4,6},{6,4},{5,7},{7,5},{8,10},{10,8},{9,1... | collective-permute-start | bytes 1105928 | tf_op jit(solution)/shard_map/ppermute | solution.py:344
  149.7 11.2 %collective-permute-start.39 = (f16[160,1152]{1,0:T(8,128)(2,1)S(1)}, f16[160,1152]{1,0:T(8,128)(2,1)S(1)}, u32[]{:S(2)}, u32[]{:S(2)}) collective-permute-start(f16[160,1152]{1,0:T(8,128)(2,1)S(1)} %add_convert_fusion), channel_id=1, source_target_pairs={{0,64},{64,0},{1,65},{65,1},{2,66},{66,2},{3,67},{67,3},{4,68},{68... | collective-permute-start | bytes 1105928 | tf_op jit(solution)/shard_map/ppermute | solution.py:344
  150.7 11.5 %collective-permute-start.38 = (f16[160,1152]{1,0:T(8,128)(2,1)S(1)}, f16[160,1152]{1,0:T(8,128)(2,1)S(1)}, u32[]{:S(2)}, u32[]{:S(2)}) collective-permute-start(f16[160,1152]{1,0:T(8,128)(2,1)S(1)} %get-tuple-element.73), channel_id=1, source_target_pairs={{0,16},{16,32},{32,48},{48,0},{1,17},{17,33},{33,49},{49,1},{2,18}... | collective-permute-start | bytes 1105928 | tf_op jit(solution)/shard_map/ppermute | solution.py:331
  152.3 17.9 %collective-permute-start.40 = (f16[160,1152]{1,0:T(8,128)(2,1)S(1)}, f16[160,1152]{1,0:T(8,128)(2,1)S(1)}, u32[]{:S(2)}, u32[]{:S(2)}) collective-permute-start(f16[160,1152]{1,0:T(8,128)(2,1)S(1)} %get-tuple-element.79), channel_id=1, source_target_pairs={{0,12},{4,0},{8,4},{12,8},{1,13},{5,1},{9,5},{13,9},{2,14},{6,2},{... | collective-permute-start | bytes 1105928 | tf_op jit(solution)/shard_map/ppermute | solution.py:331
  (25 other events, 178.7 us)
where the time goes:
time: 179 us; the launch traced here: 176 us
  starting transfers between devices  59.8 us (33%)
  waiting for transfers between devices  51.7 us (29%)
  Pallas kernels  46.7 us (26%)
  other arithmetic  6.98 us (4%)
  between operations  6.19 us (3%)
  local copies, waits for them, and re-layouts  5.1 us (3%)
    pallas_call x8, Pallas kernels, vmem_call(): pl.pallas_call(kernel, in_specs=[pl.BlockSpec(memory_space=pltpu.SMEM)] *...  46.7 us
    ppermute x22, starting transfers between devices, ring_shift(): lax.ppermute(value, axis, [(i, (i + step) % RING) for i in range(RING)])  35.4 us
    ppermute x14, waiting for transfers between devices, swap(): return lax.ppermute(value, axis, [(0, 1), (1, 0)])  18.8 us
    ppermute x22, waiting for transfers between devices, ring_shift(): lax.ppermute(value, axis, [(i, (i + step) % RING) for i in range(RING)])  17.9 us
    ppermute x7, waiting for transfers between devices, ring_split(): return lax.ppermute(value, (axis, 'core'), pairs)  14.9 us
    ppermute x14, starting transfers between devices, swap(): return lax.ppermute(value, axis, [(0, 1), (1, 0)])  13.5 us
    ppermute x7, starting transfers between devices, ring_split(): return lax.ppermute(value, (axis, 'core'), pairs)  11 us
    unnamed x12, local copies, waits for them, and re-layouts  4.37 us
  transfers between devices with their start and end apart: 43, of which 17 were waited for; matrix products, arithmetic and copies ran while one was open for 3% of the time, Pallas kernels for 17%

commit v1 on v0

--- a/solution.py
+++ b/solution.py
@@ -1,3 +1,4 @@
+import functools
 import math
 
 import jax
@@ -165,47 +166,40 @@
     return jnp.concatenate(parts, axis=0)
 
 
-def ring_merge_call(row, rows_in, col, cols_in):
+def merge_call(row, row_in, row_order, col, col_in, col_order, loss_scale, name):
+    arrays = [row, row_in] + ([] if col is None else [col, col_in])
+    pairs = [(row, row_order, 0)] + ([] if col is None else [(col, col_order, 2)])
+    out_shape = []
+    for stat, _, k in pairs:
+        done = loss_scale[k // 2] is not None
+        out_shape += [f32(*stat.shape[1:]), f32(1, stat.shape[2])] if done else [f32(*stat.shape)]
+
     def kernel(*refs):
-        row_refs, col_refs = refs[:RING], refs[RING:2 * RING]
-        for own, out in ((row_refs, refs[-2]), (col_refs, refs[-1])):
-            planes = out.shape[0]
-            stats = [[own[0][k] for k in range(planes)]]
-            for step in range(1, RING):
-                stats.append([turned(own[step], k, step) for k in range(planes)])
-            for k, value in enumerate(merge(stats)):
-                out[k] = value
-
-    return vmem_call(kernel, [f32(*row.shape), f32(*col.shape)], "merge_ring", 0, 0, [],
-                     row, *rows_in, col, *cols_in)
-
-
-def pair_merge_call(row, row_in, col, col_in, loss_scale):
-    half = col.shape[1] // 2
-
-    def kernel(row_ref, row_in_ref, col_ref, col_in_ref, row_out, lse_ref, loss_ref):
-        planes = range(row_ref.shape[0])
-        for k, value in enumerate(merge([
-                [row_ref[k] for k in planes], [swapped(row_in_ref, k, row_ref.shape[1] // 2) for k in planes]])):
-            row_out[k] = value
-        top, total = merge([[col_ref[k] for k in range(2)], [swapped(col_in_ref, k, half) for k in range(2)]])
-        lse = top + jnp.log2(total)
-        lse_ref[...] = lse
-        loss_ref[...] = jnp.sum(lse, axis=0, keepdims=True) * loss_scale
-
-    return vmem_call(kernel, [f32(*row.shape), f32(*col.shape[1:]), f32(1, col.shape[2])], "merge_pair", 0, 0, [],
-                     row, row_in, col, col_in)
-
-
-def core_merge_call(row, row_in, loss_scale):
-    def kernel(row_ref, row_in_ref, lse_ref, loss_ref):
-        planes = range(row_ref.shape[0])
-        top, total, own = merge([[row_ref[k] for k in planes], [swapped(row_in_ref, k, RING) for k in planes]])
-        lse = top + jnp.log2(total)
-        lse_ref[...] = lse
-        loss_ref[...] = jnp.sum(lse - 2.0 * own, axis=0, keepdims=True) * loss_scale
-
-    return vmem_call(kernel, [f32(*row.shape[1:]), f32(1, row.shape[2])], "merge_core", 0, 0, [], row, row_in)
+        outs = list(refs[len(arrays):])
+        for stat, order, k in pairs:
+            planes = range(stat.shape[0])
+            merged = merge([[refs[k][p] for p in planes], [order(refs[k + 1], p) for p in planes]])
+            if loss_scale[k // 2] is None:
+                out = outs.pop(0)
+                for p in planes:
+                    out[p] = merged[p]
+            else:
+                lse = merged[0] + jnp.log2(merged[1])
+                outs.pop(0)[...] = lse
+                own = 2.0 * merged[2] if len(merged) > 2 else 0.0
+                outs.pop(0)[...] = jnp.sum(lse - own, axis=0, keepdims=True) * loss_scale[k // 2]
+
+    return vmem_call(kernel, out_shape, name, 0, 0, [], *arrays)
+
+
+def join_call(parts, name):
+    def kernel(*refs):
+        at = 0
+        for ref in refs[:-1]:
+            refs[-1][pl.ds(at, ref.shape[0]), :] = ref[...]
+            at += ref.shape[0]
+
+    return vmem_call(kernel, [bf16(sum(p.shape[0] for p in parts), parts[0].shape[1])], name, 0, 0, [], *parts)[0]
 
 
 def soft_weights(v, row_lse, col_lse, first_id, col_ids):
@@ -344,10 +338,10 @@
     return lax.ppermute(value, axis, [(0, 1), (1, 0)])
 
 
-def ring_gather(value, axis, core):
+def ring_gather(value, axis, first_core, wait_for=None):
     one = ring_shift(value, axis, 1)
     three = ring_shift(value, axis, 3)
-    two = ring_split(jnp.where(core == 0, one, three), axis, 1)
+    two = ring_split(jnp.where(first_core, one, three if wait_for is None else after(three, wait_for)), axis, 1)
     return [value, one, two, three]
 
 
@@ -355,10 +349,10 @@
     return own + other.astype(jnp.float32)
 
 
-def ring_outgoing(one, three, through, core):
+def ring_outgoing(one, three, through, first_core):
     through = through.astype(jnp.float32)
-    left = one + jnp.where(core == 0, through, 0.0)
-    right = three + jnp.where(core == 0, 0.0, through)
+    left = one + jnp.where(first_core, through, 0.0)
+    right = three + jnp.where(first_core, 0.0, through)
     return left.astype(jnp.float16), right.astype(jnp.float16)
 
 
@@ -371,31 +365,39 @@
     rows = image.shape[0]
     core = lax.axis_index("core")
     place = [lax.axis_index(axis).reshape(1) for axis in AXES]
+    scale = (inverse_temp * jnp.float32(math.log2(math.e))).reshape(1)
+    image, text, scale, place, first_core = lax.optimization_barrier((image, text, scale, place, core == 0))
 
     text_far = swap(text, "ylo")
-    image = after(image, text_far)
     image_far = swap(image, "yhi")
-    text_near_slots = ring_gather(text, "z", core)
-    text_far_slots = ring_gather(text_far, "z", core)
-    image_near_slots = ring_gather(image, "x", core)
-    image_far_slots = ring_gather(image_far, "x", core)
-    image_near_other = swap(jnp.concatenate(image_near_slots), "core")
+    text_near_slots = ring_gather(text, "z", first_core)
+    text_near = join_call(text_near_slots, "join_text")
+    text_far_slots = ring_gather(text_far, "z", first_core, text_near)
+    image_near_slots = ring_gather(image, "x", first_core)
+    image_far_slots = ring_gather(image_far, "x", first_core)
+    image_near = join_call(image_near_slots, "join_image")
+    image_near_other = swap(image_near, "core")
     image_far_other = [swap(a, "core") for a in image_far_slots]
 
-    scale = (inverse_temp * jnp.float32(math.log2(math.e))).reshape(1)
     s_near, x_near, row_stat, col_stat, t_all = score_call(
-        image_near_slots + [image_near_other], text_near_slots + text_far_slots, scale, place, 0, [], rows,
-        "score_near")
+        [image_near, image_near_other], [text_near] + text_far_slots, scale, place, 0, [], rows, "score_near")
     s_far, x_far, row_stat, col_stat = score_call(
         image_far_slots + image_far_other, [t_all], scale, place, 1, [row_stat, col_stat], rows, "score_far")
 
     loss_scale = math.log(2.0) / (2 * 128 * rows)
-    row_stat, col_stat = ring_merge_call(
-        row_stat, [ring_shift(row_stat, "x", step) for step in (1, 2, 3)],
-        col_stat, [ring_shift(col_stat, "z", step) for step in (1, 2, 3)])
-    row_stat, col_lse, col_loss = pair_merge_call(
-        row_stat, swap(row_stat, "yhi"), col_stat, swap(col_stat, "ylo"), loss_scale)
-    row_lse, row_loss = core_merge_call(row_stat, swap(row_stat, "core"), loss_scale)
+    one, two = (functools.partial(turned, step=step) for step in (1, 2))
+    cores, pairs = functools.partial(swapped, group=RING), functools.partial(swapped, group=2 * RING)
+    row_stat, col_stat = merge_call(
+        row_stat, swap(row_stat, "core"), cores, col_stat, ring_shift(col_stat, "z", 1), one,
+        (None, None), "merge_core")
+    row_stat, col_stat = merge_call(
+        row_stat, ring_shift(row_stat, "x", 1), one, col_stat, ring_shift(col_stat, "z", 2), two,
+        (None, None), "merge_one")
+    row_stat, col_lse, col_loss = merge_call(
+        row_stat, ring_shift(row_stat, "x", 2), two, col_stat, swap(col_stat, "ylo"), cores,
+        (None, loss_scale), "merge_two")
+    row_lse, row_loss = merge_call(
+        row_stat, swap(row_stat, "yhi"), pairs, None, None, None, (loss_scale,), "merge_pair")
 
     w_far, far_own, far_part = image_call(s_far, row_lse, col_lse, col_loss, place, t_all, rows, "image_far")
     far_send = far_part.astype(jnp.float16)
@@ -409,26 +411,27 @@
     far_through = ring_split(far_two, "x", -1)
     near_own, near_part = near_call(after(w_near, far_two), t_all, col_loss, rows, "image_near")
     near_send = near_part.astype(jnp.float16)
-    near_other = swap(near_send, "core")
-
+
+    through, _, through_two = lax.optimization_barrier((far_through, near_send, text_through))
     far_left, far_right = ring_outgoing(
-        summed(far_own[1], far_other[1]), summed(far_own[3], far_other[3]), after(far_through, near_send), core)
-    far_text_left, far_text_right = ring_outgoing(
-        far_text[1], far_text[3], after(text_through, far_left)[1], core)
-    near_two = summed(near_own[2], after(near_other, far_text_left)[2]).astype(jnp.float16)
+        summed(far_own[1], far_other[1]), summed(far_own[3], far_other[3]), through, first_core)
+    near_other = swap(after(near_send, far_left), "core")
+    text_left, text_right = ring_outgoing(
+        far_text[1], far_text[3], after(through_two, far_left)[1], first_core)
+    near_two = summed(near_own[2], after(near_other, text_left)[2]).astype(jnp.float16)
     near_through = ring_split(near_two, "x", -1)
+    image_far_sum = ring_arrived(
+        summed(far_own[0], after(far_other, near_two)[0]), far_left, far_right, "x").astype(jnp.float16)
+    image_far_in = swap(image_far_sum, "yhi")
+    near_left, near_right = ring_outgoing(
+        summed(near_own[1], near_other[1]), summed(near_own[3], near_other[3]),
+        after(near_through, image_far_sum), first_core)
+    text_far_sum = ring_arrived(after(far_text[0], near_left), text_left, text_right, "z").astype(jnp.float16)
     near_text_left, near_text_right = ring_outgoing(
-        near_text[1], near_text[3], after(text_through, near_two)[0], core)
-    image_far_sum = ring_arrived(
-        summed(far_own[0], after(far_other, near_text_left)[0]), far_left, far_right, "x").astype(jnp.float16)
-    text_far_sum = ring_arrived(
-        after(far_text[0], image_far_sum), far_text_left, far_text_right, "z").astype(jnp.float16)
-    near_left, near_right = ring_outgoing(
-        summed(near_own[1], near_other[1]), summed(near_own[3], near_other[3]), after(near_through, text_far_sum), core)
-    text_sum = (ring_arrived(after(near_text[0], near_left), near_text_left, near_text_right, "z")
-                + swap(text_far_sum, "ylo").astype(jnp.float32))
+        near_text[1], near_text[3], after(through_two, image_far_sum)[0], first_core)
     image_sum = (ring_arrived(summed(near_own[0], near_other[0]), near_left, near_right, "x")
-                 + swap(image_far_sum, "yhi").astype(jnp.float32))
+                 + image_far_in.astype(jnp.float32))
+    text_sum = ring_arrived(near_text[0], near_text_left, near_text_right, "z") + swap(text_far_sum, "ylo").astype(jnp.float32)
 
     digits = text_sum[rows:, 0] + image_sum[rows:, 0]
     loss_value = sum(digits[k] * unit for k, unit in enumerate(UNITS))

time: 179 us -> 168 us (0.939)
  starting transfers between devices: 59.8 us -> 44.6 us
  waiting for transfers between devices: 51.7 us -> 65.3 us
  local copies, waits for them, and re-layouts: 5.1 us -> 1.69 us
  Pallas kernels: 46.7 us -> 43.3 us
  other arithmetic: 6.98 us -> 4.96 us
    ppermute x22 -> x20, waiting for transfers between devices: 17.9 us -> 34.6 us  [ring_shift(): lax.ppermute(value, axis, [(i, (i + step) % RING) for i in range(RING)])]
    ppermute x14, waiting for transfers between devices: 18.8 us -> 7.6 us  [swap(): return lax.ppermute(value, axis, [(0, 1), (1, 0)])]
    ppermute x7, starting transfers between devices: 11 us -> 1.2 us  [ring_split(): return lax.ppermute(value, (axis, 'core'), pairs)]
    ppermute x7, waiting for transfers between devices: 14.9 us -> 23.1 us  [ring_split(): return lax.ppermute(value, (axis, 'core'), pairs)]
    ppermute x22 -> x20, starting transfers between devices: 35.4 us -> 31 us  [ring_shift(): lax.ppermute(value, axis, [(i, (i + step) % RING) for i in range(RING)])]
    pallas_call x8 -> x11, Pallas kernels: 46.7 us -> 43.3 us  [vmem_call(): pl.pallas_call(kernel, in_specs=[pl.BlockSpec(memory_space=pltpu.SMEM)] *...]
    unnamed x12 -> x4, local copies, waits for them, and re-layouts: 4.37 us -> 0.98 us
    concatenate x1 -> x0, other arithmetic: 2.15 us -> none  [on_device(): image_near_other = swap(jnp.concatenate(image_near_slots), 'core')]
  transfers between devices with their start and end apart: 43 -> 41, of which waited for: 17 -> 16; matrix products, arithmetic and copies ran while one was open for 3% -> 2% of each run, Pallas kernels for 17% -> 20%
where the time goes in v1:
time: 168 us; the launch traced here: 166 us
  waiting for transfers between devices  65.3 us (39%)
  starting transfers between devices  44.6 us (27%)
  Pallas kernels  43.3 us (26%)
  between operations  6.17 us (4%)
  other arithmetic  4.96 us (3%)
  local copies, waits for them, and re-layouts  1.69 us (1%)
    pallas_call x11, Pallas kernels, vmem_call(): pl.pallas_call(kernel, in_specs=[pl.BlockSpec(memory_space=pltpu.SMEM)] *...  43.3 us
    ppermute x20, waiting for transfers between devices, ring_shift(): lax.ppermute(value, axis, [(i, (i + step) % RING) for i in range(RING)])  34.6 us
    ppermute x20, starting transfers between devices, ring_shift(): lax.ppermute(value, axis, [(i, (i + step) % RING) for i in range(RING)])  31 us
    ppermute x7, waiting for transfers between devices, ring_split(): return lax.ppermute(value, (axis, 'core'), pairs)  23.1 us
    ppermute x14, starting transfers between devices, swap(): return lax.ppermute(value, axis, [(0, 1), (1, 0)])  12.4 us
    ppermute x14, waiting for transfers between devices, swap(): return lax.ppermute(value, axis, [(0, 1), (1, 0)])  7.6 us
  transfers between devices with their start and end apart: 41, of which 16 were waited for; matrix products, arithmetic and copies ran while one was open for 2% of the time, Pallas kernels for 20%

profile of v1, /device:TPU:0, one launch (start us, length us, event | category | flops | bytes accessed | tf_op | source)
XLA Modules:
  0.0 165.9 jit_solution(4177120617924833311)
XLA Ops:
  1.4 2.9 %collective-permute-start.1 = (bf16[144,1152]{1,0:T(8,128)(2,1)}, bf16[144,1152]{1,0:T(8,128)(2,1)S(1)}, u32[]{:S(2)}, u32[]{:S(2)}) collective-permute-start(bf16[144,1152]{1,0:T(8,128)(2,1)} %refs_0_), channel_id=1, source_target_pairs={{0,12},{4,0},{8,4},{12,8},{1,13},{5,1},{9,5},{13,9},{2,14},{6,2},{... | collective-permute-start | bytes 995336 | tf_op jit(solution)/shard_map/ppermute | solution.py:325
  4.3 3.2 %collective-permute-start.11 = (bf16[144,1152]{1,0:T(8,128)(2,1)}, bf16[144,1152]{1,0:T(8,128)(2,1)S(1)}, u32[]{:S(2)}, u32[]{:S(2)}) collective-permute-start(bf16[144,1152]{1,0:T(8,128)(2,1)} %refs_0_), channel_id=1, source_target_pairs={{0,2},{2,0},{1,3},{3,1},{4,6},{6,4},{5,7},{7,5},{8,10},{10,8},{9,1... | collective-permute-start | bytes 995336 | tf_op jit(solution)/shard_map/ppermute | solution.py:338
  8.2 4.0 %collective-permute-start.5 = (bf16[144,1152]{1,0:T(8,128)(2,1)}, bf16[144,1152]{1,0:T(8,128)(2,1)S(1)}, u32[]{:S(2)}, u32[]{:S(2)}) collective-permute-start(bf16[144,1152]{1,0:T(8,128)(2,1)} %refs_0_.1), channel_id=1, source_target_pairs={{0,48},{16,0},{32,16},{48,32},{1,49},{17,1},{33,17},{49,33},{2,50}... | collective-permute-start | bytes 995336 | tf_op jit(solution)/shard_map/ppermute | solution.py:325
  16.7 3.2 %collective-permute-start.13 = (bf16[144,1152]{1,0:T(8,128)(2,1)S(1)}, bf16[144,1152]{1,0:T(8,128)(2,1)S(1)}, u32[]{:S(2)}, u32[]{:S(2)}) collective-permute-start(bf16[144,1152]{1,0:T(8,128)(2,1)S(1)} %collective-permute-done.11.refs_5_), channel_id=1, source_target_pairs={{0,12},{4,0},{8,4},{12,8},{1,13},{5,1},{9,5},{13,9},{2,14},{6,2},{... | collective-permute-start | bytes 995336 | tf_op jit(solution)/shard_map/ppermute | solution.py:325
  20.0 2.9 %collective-permute-done.4.refs_1_ = bf16[144,1152]{1,0:T(8,128)(2,1)S(1)} collective-permute-done((bf16[144,1152]{1,0:T(8,128)(2,1)}, bf16[144,1152]{1,0:T(8,128)(2,1)S(1)}, u32[]{:S(2)}, u32[]{:S(2)}) %collective-permute-start.4) | collective-permute-done | bytes 331808 | tf_op jit(solution)/shard_map/ppermute | solution.py:325
  23.0 3.8 %collective-permute-start.9 = (bf16[144,1152]{1,0:T(8,128)(2,1)S(1)}, bf16[144,1152]{1,0:T(8,128)(2,1)S(1)}, u32[]{:S(2)}, u32[]{:S(2)}) collective-permute-start(bf16[144,1152]{1,0:T(8,128)(2,1)S(1)} %collective-permute-done.7.refs_8_), channel_id=1, source_target_pairs={{0,48},{16,0},{32,16},{48,32},{1,49},{17,1},{33,17},{49,33},{2,50}... | collective-permute-start | bytes 995336 | tf_op jit(solution)/shard_map/ppermute | solution.py:325
  30.7 2.9 %collective-permute-done.6.refs_2_ = bf16[144,1152]{1,0:T(8,128)(2,1)S(1)} collective-permute-done((bf16[144,1152]{1,0:T(8,128)(2,1)S(1)}, bf16[144,1152]{1,0:T(8,128)(2,1)S(1)}, u32[]{:S(2)}, u32[]{:S(2)}) %collective-permute-start.6) | collective-permute-done | bytes 331808 | tf_op jit(solution)/shard_map/ppermute | solution.py:334
  33.8 4.6 %collective-permute-done.8.refs_9_ = bf16[144,1152]{1,0:T(8,128)(2,1)S(1)} collective-permute-done((bf16[144,1152]{1,0:T(8,128)(2,1)S(1)}, bf16[144,1152]{1,0:T(8,128)(2,1)S(1)}, u32[]{:S(2)}, u32[]{:S(2)}) %collective-permute-start.8) | collective-permute-done | bytes 331808 | tf_op jit(solution)/shard_map/ppermute | solution.py:325
  39.2 7.6 %collective-permute-done.10.refs_10_ = bf16[144,1152]{1,0:T(8,128)(2,1)S(1)} collective-permute-done((bf16[144,1152]{1,0:T(8,128)(2,1)S(1)}, bf16[144,1152]{1,0:T(8,128)(2,1)S(1)}, u32[]{:S(2)}, u32[]{:S(2)}) %collective-permute-start.10) | collective-permute-done | bytes 331808 | tf_op jit(solution)/shard_map/ppermute | solution.py:334
  46.8 17.9 %score_near.1 = (f32[1152,1152]{1,0:T(8,128)S(1)}, bf16[1152,1152]{1,0:T(8,128)(2,1)S(1)}, f32[3,8,144]{2,1,0:T(8,128)S(1)}, f32[2,8,144]{2,1,0:T(8,128)S(1)}, bf16[1152,1152]{1,0:T(8,128)(2,1)S(1)}) custom-call(f32[1]{0:T(128)} %bitcast.scale_ref, s32[1]{0:T(128)} %bitcast.1.refs_0_, s32[1]{0:T(128)} %bitcast.2.refs_1_, s32[1]{0:T(128)} %bitcast.3.refs_2_, ...), custom_call_target="tpu_custom_call" | custom-call | flops 3057647616 | bytes 15948288 | tf_op jit(solution)/shard_map/score_near/pallas_call | solution.py:31
  64.8 5.2 %score_far.1 = (f32[1152,1152]{1,0:T(8,128)S(1)}, bf16[1152,1152]{1,0:T(8,128)(2,1)S(1)}, f32[3,16,144]{2,1,0:T(8,128)S(1)}, f32[2,8,144]{2,1,0:T(8,128)S(1)}) custom-call(f32[1]{0:T(128)} %bitcast.scale_ref, s32[1]{0:T(128)} %bitcast.1.refs_0_, s32[1]{0:T(128)} %bitcast.2.refs_1_, s32[1]{0:T(128)} %bitcast.3.refs_2_, s32[1]{0:T(128)} %bitcast.4.refs_3_, ...), custom_call_target="tpu_custom_call" | custom-call | flops 3057647616 | bytes 13330944 | tf_op jit(solution)/shard_map/score_far/pallas_call | solution.py:31
  70.3 4.9 %collective-permute-done.20.refs_3_ = f32[2,8,144]{2,1,0:T(8,128)S(1)} collective-permute-done((f32[2,8,144]{2,1,0:T(8,128)S(1)}, f32[2,8,144]{2,1,0:T(8,128)S(1)}, u32[]{:S(2)}, u32[]{:S(2)}) %collective-permute-start.20) | collective-permute-done | bytes 9248 | tf_op jit(solution)/shard_map/ppermute | solution.py:325
  76.4 5.2 %collective-permute-done.22.refs_3_ = f32[2,8,144]{2,1,0:T(8,128)S(1)} collective-permute-done((f32[2,8,144]{2,1,0:T(8,128)S(1)}, f32[2,8,144]{2,1,0:T(8,128)S(1)}, u32[]{:S(2)}, u32[]{:S(2)}) %collective-permute-start.22) | collective-permute-done | bytes 9248 | tf_op jit(solution)/shard_map/ppermute | solution.py:325
  81.7 4.0 %collective-permute-start.23 = (f32[3,16,144]{2,1,0:T(8,128)S(1)}, f32[3,16,144]{2,1,0:T(8,128)S(1)}, u32[]{:S(2)}, u32[]{:S(2)}) collective-permute-start(f32[3,16,144]{2,1,0:T(8,128)S(1)} %get-tuple-element.68.refs_0_), channel_id=1, source_target_pairs={{0,8},{4,12},{8,0},{12,4},{1,9},{5,13},{9,1},{13,5},{2,10},{6,14},... | collective-permute-start | bytes 82952 | tf_op jit(solution)/shard_map/ppermute | solution.py:325
  91.7 3.6 %collective-permute-done.25.refs_1_ = f32[3,16,144]{2,1,0:T(8,128)S(1)} collective-permute-done((f32[3,16,144]{2,1,0:T(8,128)S(1)}, f32[3,16,144]{2,1,0:T(8,128)S(1)}, u32[]{:S(2)}, u32[]{:S(2)}) %collective-permute-start.25) | collective-permute-done | bytes 27680 | tf_op jit(solution)/shard_map/ppermute | solution.py:338
  95.4 5.2 %image_far.1 = (bf16[1152,1152]{1,0:T(8,128)(2,1)S(1)}, f32[4,160,1152]{2,1,0:T(8,128)S(1)}, f32[4,160,1152]{2,1,0:T(8,128)S(1)}) custom-call(s32[1]{0:T(128)} %bitcast.1.refs_0_, s32[1]{0:T(128)} %bitcast.2.refs_1_, s32[1]{0:T(128)} %bitcast.3.refs_2_, s32[1]{0:T(128)} %bitcast.4.refs_3_, s32[1]{0:T(128)} %bitcast.5.refs_4_, ...), custom_call_target="tpu_custom_call" | custom-call | flops 3057647616 | bytes 16529472 | tf_op jit(solution)/shard_map/image_far/pallas_call | solution.py:31
  101.2 10.7 %text_all.1 = (bf16[1152,1152]{1,0:T(8,128)(2,1)S(1)}, f32[8,160,1152]{2,1,0:T(8,128)S(1)}) custom-call(s32[1]{0:T(128)} %bitcast.1.refs_0_, s32[1]{0:T(128)} %bitcast.2.refs_1_, s32[1]{0:T(128)} %bitcast.3.refs_2_, s32[1]{0:T(128)} %bitcast.4.refs_3_, s32[1]{0:T(128)} %bitcast.5.refs_4_, f32[1152,1152]{1,0:T(8,128)S(1)} %get-tuple-element.60.refs_5_, ...), custom_call_target="tpu_custom_call" | custom-call | flops 6115295232 | bytes 21837888 | tf_op jit(solution)/shard_map/text_all/pallas_call | solution.py:31
  113.4 3.9 %image_near.1 = (f32[4,160,1152]{2,1,0:T(8,128)S(1)}, f32[4,160,1152]{2,1,0:T(8,128)S(1)}) custom-call(bf16[1152,1152]{1,0:T(8,128)(2,1)S(1)} %get-tuple-element.85.w_ref, bf16[1152,1152]{1,0:T(8,128)(2,1)S(1)} %get-tuple-element.61.refs_13_.refs_9_.t_ref, f32[1,144]{1,0:T(1,128)S(1)} %get-tuple-element.74.refs_8_.loss_ref), custom_call_target="tpu_custom_call" | custom-call | flops 3057647616 | bytes 11207232 | tf_op jit(solution)/shard_map/image_near/pallas_call | solution.py:31
  117.5 6.7 %collective-permute-done.28 = f16[2,160,1152]{2,1,0:T(8,128)(2,1)S(1)} collective-permute-done((f16[2,160,1152]{2,1,0:T(8,128)(2,1)S(1)}, f16[2,160,1152]{2,1,0:T(8,128)(2,1)S(1)}, u32[]{:S(2)}, u32[]{:S(2)}) %collective-permute-start.28) | collective-permute-done | bytes 737312 | tf_op jit(solution)/shard_map/ppermute | solution.py:334
  127.5 3.2 %collective-permute-start.35 = (f16[160,1152]{1,0:T(8,128)(2,1)S(1)}, f16[160,1152]{1,0:T(8,128)(2,1)S(1)}, u32[]{:S(2)}, u32[]{:S(2)}) collective-permute-start(f16[160,1152]{1,0:T(8,128)(2,1)S(1)} %get-tuple-element.100), channel_id=1, source_target_pairs={{0,48},{16,0},{32,16},{48,32},{1,49},{17,1},{33,17},{49,33},{2,50}... | collective-permute-start | bytes 1105928 | tf_op jit(solution)/shard_map/ppermute | solution.py:325
  130.8 6.2 %collective-permute-done.31 = f16[160,1152]{1,0:T(8,128)(2,1)S(1)} collective-permute-done((f16[160,1152]{1,0:T(8,128)(2,1)S(1)}, f16[160,1152]{1,0:T(8,128)(2,1)S(1)}, u32[]{:S(2)}, u32[]{:S(2)}) %collective-permute-start.31) | collective-permute-done | bytes 368672 | tf_op jit(solution)/shard_map/ppermute | solution.py:325
  137.3 2.6 %collective-permute-start.40 = (f16[160,1152]{1,0:T(8,128)(2,1)S(1)}, f16[160,1152]{1,0:T(8,128)(2,1)S(1)}, u32[]{:S(2)}, u32[]{:S(2)}) collective-permute-start(f16[160,1152]{1,0:T(8,128)(2,1)S(1)} %fusion.19), channel_id=1, source_target_pairs={{0,2},{2,0},{1,3},{3,1},{4,6},{6,4},{5,7},{7,5},{8,10},{10,8},{9,1... | collective-permute-start | bytes 1105928 | tf_op jit(solution)/shard_map/ppermute | solution.py:338
  141.6 5.8 %collective-permute-done.34 = f16[160,1152]{1,0:T(8,128)(2,1)S(1)} collective-permute-done((f16[160,1152]{1,0:T(8,128)(2,1)S(1)}, f16[160,1152]{1,0:T(8,128)(2,1)S(1)}, u32[]{:S(2)}, u32[]{:S(2)}) %collective-permute-start.34) | collective-permute-done | bytes 368672 | tf_op jit(solution)/shard_map/ppermute | solution.py:334
  150.1 8.5 %collective-permute-done.39 = f16[160,1152]{1,0:T(8,128)(2,1)S(1)} collective-permute-done((f16[160,1152]{1,0:T(8,128)(2,1)S(1)}, f16[160,1152]{1,0:T(8,128)(2,1)S(1)}, u32[]{:S(2)}, u32[]{:S(2)}) %collective-permute-start.39) | collective-permute-done | bytes 368672 | tf_op jit(solution)/shard_map/ppermute | solution.py:325
  (96 shorter events, 30.7 us)
Async XLA Ops:
  1.4 10.8 %collective-permute-start.1 = (bf16[144,1152]{1,0:T(8,128)(2,1)}, bf16[144,1152]{1,0:T(8,128)(2,1)S(1)}, u32[]{:S(2)}, u32[]{:S(2)}) collective-permute-start(bf16[144,1152]{1,0:T(8,128)(2,1)} %refs_0_), channel_id=1, source_target_pairs={{0,12},{4,0},{8,4},{12,8},{1,13},{5,1},{9,5},{13,9},{2,14},{6,2},{... | collective-permute-start | bytes 995336 | tf_op jit(solution)/shard_map/ppermute | solution.py:325
  4.3 12.4 %collective-permute-start.11 = (bf16[144,1152]{1,0:T(8,128)(2,1)}, bf16[144,1152]{1,0:T(8,128)(2,1)S(1)}, u32[]{:S(2)}, u32[]{:S(2)}) collective-permute-start(bf16[144,1152]{1,0:T(8,128)(2,1)} %refs_0_), channel_id=1, source_target_pairs={{0,2},{2,0},{1,3},{3,1},{4,6},{6,4},{5,7},{7,5},{8,10},{10,8},{9,1... | collective-permute-start | bytes 995336 | tf_op jit(solution)/shard_map/ppermute | solution.py:338
  7.5 15.5 %collective-permute-start.7 = (bf16[144,1152]{1,0:T(8,128)(2,1)}, bf16[144,1152]{1,0:T(8,128)(2,1)S(1)}, u32[]{:S(2)}, u32[]{:S(2)}) collective-permute-start(bf16[144,1152]{1,0:T(8,128)(2,1)} %refs_0_.1), channel_id=1, source_target_pairs={{0,64},{64,0},{1,65},{65,1},{2,66},{66,2},{3,67},{67,3},{4,68},{68... | collective-permute-start | bytes 995336 | tf_op jit(solution)/shard_map/ppermute | solution.py:338
  8.2 11.8 %collective-permute-start.5 = (bf16[144,1152]{1,0:T(8,128)(2,1)}, bf16[144,1152]{1,0:T(8,128)(2,1)S(1)}, u32[]{:S(2)}, u32[]{:S(2)}) collective-permute-start(bf16[144,1152]{1,0:T(8,128)(2,1)} %refs_0_.1), channel_id=1, source_target_pairs={{0,48},{16,0},{32,16},{48,32},{1,49},{17,1},{33,17},{49,33},{2,50}... | collective-permute-start | bytes 995336 | tf_op jit(solution)/shard_map/ppermute | solution.py:325
  15.0 11.7 %collective-permute-start.2 = (bf16[144,1152]{1,0:T(8,128)(2,1)S(1)}, bf16[144,1152]{1,0:T(8,128)(2,1)S(1)}, u32[]{:S(2)}, u32[]{:S(2)}) collective-permute-start(bf16[144,1152]{1,0:T(8,128)(2,1)S(1)} %broadcast_select_fusion.3), channel_id=1, source_target_pairs={{0,4},{1,13},{4,8},{5,1},{8,12},{9,5},{12,0},{13,9},{2,6},{3,15},{... | collective-permute-start | bytes 995336 | tf_op jit(solution)/shard_map/ppermute | solution.py:334
  16.7 13.0 %collective-permute-start.13 = (bf16[144,1152]{1,0:T(8,128)(2,1)S(1)}, bf16[144,1152]{1,0:T(8,128)(2,1)S(1)}, u32[]{:S(2)}, u32[]{:S(2)}) collective-permute-start(bf16[144,1152]{1,0:T(8,128)(2,1)S(1)} %collective-permute-done.11.refs_5_), channel_id=1, source_target_pairs={{0,12},{4,0},{8,4},{12,8},{1,13},{5,1},{9,5},{13,9},{2,14},{6,2},{... | collective-permute-start | bytes 995336 | tf_op jit(solution)/shard_map/ppermute | solution.py:325
  23.0 10.8 %collective-permute-start.9 = (bf16[144,1152]{1,0:T(8,128)(2,1)S(1)}, bf16[144,1152]{1,0:T(8,128)(2,1)S(1)}, u32[]{:S(2)}, u32[]{:S(2)}) collective-permute-start(bf16[144,1152]{1,0:T(8,128)(2,1)S(1)} %collective-permute-done.7.refs_8_), channel_id=1, source_target_pairs={{0,48},{16,0},{32,16},{48,32},{1,49},{17,1},{33,17},{49,33},{2,50}... | collective-permute-start | bytes 995336 | tf_op jit(solution)/shard_map/ppermute | solution.py:325
  26.8 11.6 %collective-permute-start.8 = (bf16[144,1152]{1,0:T(8,128)(2,1)S(1)}, bf16[144,1152]{1,0:T(8,128)(2,1)S(1)}, u32[]{:S(2)}, u32[]{:S(2)}) collective-permute-start(bf16[144,1152]{1,0:T(8,128)(2,1)S(1)} %collective-permute-done.7.refs_8_), channel_id=1, source_target_pairs={{0,16},{16,32},{32,48},{48,0},{1,17},{17,33},{33,49},{49,1},{2,18}... | collective-permute-start | bytes 995336 | tf_op jit(solution)/shard_map/ppermute | solution.py:325
  29.7 17.1 %collective-permute-start.3 = (bf16[576,1152]{1,0:T(8,128)(2,1)S(1)}, bf16[576,1152]{1,0:T(8,128)(2,1)S(1)}, u32[]{:S(2)}, u32[]{:S(2)}) collective-permute-start(bf16[576,1152]{1,0:T(8,128)(2,1)S(1)} %join_image.1.refs_5_), channel_id=1, source_target_pairs={{0,1},{1,0},{2,3},{3,2},{4,5},{5,4},{6,7},{7,6},{8,9},{9,8},{10,11... | collective-permute-start | bytes 3981320 | tf_op jit(solution)/shard_map/ppermute | solution.py:338
  38.5 26.2 %collective-permute-start.15 = (bf16[144,1152]{1,0:T(8,128)(2,1)S(1)}, bf16[144,1152]{1,0:T(8,128)(2,1)S(1)}, u32[]{:S(2)}, u32[]{:S(2)}) collective-permute-start(bf16[144,1152]{1,0:T(8,128)(2,1)S(1)} %collective-permute-done.11.refs_5_), channel_id=1, source_target_pairs={{0,1},{1,0},{2,3},{3,2},{4,5},{5,4},{6,7},{7,6},{8,9},{9,8},{10,11... | collective-permute-start | bytes 995336 | tf_op jit(solution)/shard_map/ppermute | solution.py:338
  38.6 26.1 %collective-permute-start.18 = (bf16[144,1152]{1,0:T(8,128)(2,1)S(1)}, bf16[144,1152]{1,0:T(8,128)(2,1)S(1)}, u32[]{:S(2)}, u32[]{:S(2)}) collective-permute-start(bf16[144,1152]{1,0:T(8,128)(2,1)S(1)} %collective-permute-done.13.refs_8_), channel_id=1, source_target_pairs={{0,1},{1,0},{2,3},{3,2},{4,5},{5,4},{6,7},{7,6},{8,9},{9,8},{10,11... | collective-permute-start | bytes 995336 | tf_op jit(solution)/shard_map/ppermute | solution.py:338
  39.1 25.7 %collective-permute-start.16 = (bf16[144,1152]{1,0:T(8,128)(2,1)S(1)}, bf16[144,1152]{1,0:T(8,128)(2,1)S(1)}, u32[]{:S(2)}, u32[]{:S(2)}) collective-permute-start(bf16[144,1152]{1,0:T(8,128)(2,1)S(1)} %collective-permute-done.12.refs_6_), channel_id=1, source_target_pairs={{0,1},{1,0},{2,3},{3,2},{4,5},{5,4},{6,7},{7,6},{8,9},{9,8},{10,11... | collective-permute-start | bytes 995336 | tf_op jit(solution)/shard_map/ppermute | solution.py:338
  46.8 17.9 %collective-permute-start.17 = (bf16[144,1152]{1,0:T(8,128)(2,1)S(1)}, bf16[144,1152]{1,0:T(8,128)(2,1)S(1)}, u32[]{:S(2)}, u32[]{:S(2)}) collective-permute-start(bf16[144,1152]{1,0:T(8,128)(2,1)S(1)} %collective-permute-done.14.refs_7_), channel_id=1, source_target_pairs={{0,1},{1,0},{2,3},{3,2},{4,5},{5,4},{6,7},{7,6},{8,9},{9,8},{10,11... | collective-permute-start | bytes 995336 | tf_op jit(solution)/shard_map/ppermute | solution.py:338
  100.8 12.0 %collective-permute-start.26 = (f16[4,160,1152]{2,1,0:T(8,128)(2,1)S(1)}, f16[4,160,1152]{2,1,0:T(8,128)(2,1)S(1)}, u32[]{:S(2)}, u32[]{:S(2)}) collective-permute-start(f16[4,160,1152]{2,1,0:T(8,128)(2,1)S(1)} %convert_element_type.137), channel_id=1, source_target_pairs={{0,1},{1,0},{2,3},{3,2},{4,5},{5,4},{6,7},{7,6},{8,9},{9,8},{10,11... | collective-permute-start | bytes 4423688 | tf_op jit(solution)/shard_map/ppermute | solution.py:338
  112.7 11.5 %collective-permute-start.28 = (f16[2,160,1152]{2,1,0:T(8,128)(2,1)S(1)}, f16[2,160,1152]{2,1,0:T(8,128)(2,1)S(1)}, u32[]{:S(2)}, u32[]{:S(2)}) collective-permute-start(f16[2,160,1152]{2,1,0:T(8,128)(2,1)S(1)} %pad_maximum_fusion), channel_id=1, source_target_pairs={{0,48},{1,17},{16,0},{17,33},{32,16},{33,49},{48,32},{49,1},{2,50}... | collective-permute-start | bytes 2211848 | tf_op jit(solution)/shard_map/ppermute | solution.py:334
  112.9 11.3 %collective-permute-start.27 = (f16[160,1152]{1,0:T(8,128)(2,1)S(1)}, f16[160,1152]{1,0:T(8,128)(2,1)S(1)}, u32[]{:S(2)}, u32[]{:S(2)}) collective-permute-start(f16[160,1152]{1,0:T(8,128)(2,1)S(1)} %fusion.22), channel_id=1, source_target_pairs={{0,12},{1,5},{4,0},{5,9},{8,4},{9,13},{12,8},{13,1},{2,14},{3,7},{... | collective-permute-start | bytes 1105928 | tf_op jit(solution)/shard_map/ppermute | solution.py:334
  125.2 11.9 %collective-permute-start.30 = (f16[160,1152]{1,0:T(8,128)(2,1)S(1)}, f16[160,1152]{1,0:T(8,128)(2,1)S(1)}, u32[]{:S(2)}, u32[]{:S(2)}) collective-permute-start(f16[160,1152]{1,0:T(8,128)(2,1)S(1)} %get-tuple-element.104), channel_id=1, source_target_pairs={{0,12},{4,0},{8,4},{12,8},{1,13},{5,1},{9,5},{13,9},{2,14},{6,2},{... | collective-permute-start | bytes 1105928 | tf_op jit(solution)/shard_map/ppermute | solution.py:325
  125.5 11.6 %collective-permute-start.31 = (f16[160,1152]{1,0:T(8,128)(2,1)S(1)}, f16[160,1152]{1,0:T(8,128)(2,1)S(1)}, u32[]{:S(2)}, u32[]{:S(2)}) collective-permute-start(f16[160,1152]{1,0:T(8,128)(2,1)S(1)} %get-tuple-element.105), channel_id=1, source_target_pairs={{0,4},{4,8},{8,12},{12,0},{1,5},{5,9},{9,13},{13,1},{2,6},{6,10},{... | collective-permute-start | bytes 1105928 | tf_op jit(solution)/shard_map/ppermute | solution.py:325
  127.4 20.3 %collective-permute-start.36 = (f16[160,1152]{1,0:T(8,128)(2,1)S(1)}, f16[160,1152]{1,0:T(8,128)(2,1)S(1)}, u32[]{:S(2)}, u32[]{:S(2)}) collective-permute-start(f16[160,1152]{1,0:T(8,128)(2,1)S(1)} %get-tuple-element.99), channel_id=1, source_target_pairs={{0,16},{16,32},{32,48},{48,0},{1,17},{17,33},{33,49},{49,1},{2,18}... | collective-permute-start | bytes 1105928 | tf_op jit(solution)/shard_map/ppermute | solution.py:325
  127.5 21.8 %collective-permute-start.35 = (f16[160,1152]{1,0:T(8,128)(2,1)S(1)}, f16[160,1152]{1,0:T(8,128)(2,1)S(1)}, u32[]{:S(2)}, u32[]{:S(2)}) collective-permute-start(f16[160,1152]{1,0:T(8,128)(2,1)S(1)} %get-tuple-element.100), channel_id=1, source_target_pairs={{0,48},{16,0},{32,16},{48,32},{1,49},{17,1},{33,17},{49,33},{2,50}... | collective-permute-start | bytes 1105928 | tf_op jit(solution)/shard_map/ppermute | solution.py:325
  137.3 12.8 %collective-permute-start.40 = (f16[160,1152]{1,0:T(8,128)(2,1)S(1)}, f16[160,1152]{1,0:T(8,128)(2,1)S(1)}, u32[]{:S(2)}, u32[]{:S(2)}) collective-permute-start(f16[160,1152]{1,0:T(8,128)(2,1)S(1)} %fusion.19), channel_id=1, source_target_pairs={{0,2},{2,0},{1,3},{3,1},{4,6},{6,4},{5,7},{7,5},{8,10},{10,8},{9,1... | collective-permute-start | bytes 1105928 | tf_op jit(solution)/shard_map/ppermute | solution.py:338
  140.4 19.4 %collective-permute-start.32 = (f16[160,1152]{1,0:T(8,128)(2,1)S(1)}, f16[160,1152]{1,0:T(8,128)(2,1)S(1)}, u32[]{:S(2)}, u32[]{:S(2)}) collective-permute-start(f16[160,1152]{1,0:T(8,128)(2,1)S(1)} %get-tuple-element.97), channel_id=1, source_target_pairs={{0,48},{16,0},{32,16},{48,32},{1,49},{17,1},{33,17},{49,33},{2,50}... | collective-permute-start | bytes 1105928 | tf_op jit(solution)/shard_map/ppermute | solution.py:325
  147.4 12.3 %collective-permute-start.33 = (f16[160,1152]{1,0:T(8,128)(2,1)S(1)}, f16[160,1152]{1,0:T(8,128)(2,1)S(1)}, u32[]{:S(2)}, u32[]{:S(2)}) collective-permute-start(f16[160,1152]{1,0:T(8,128)(2,1)S(1)} %get-tuple-element.98), channel_id=1, source_target_pairs={{0,16},{16,32},{32,48},{48,0},{1,17},{17,33},{33,49},{49,1},{2,18}... | collective-permute-start | bytes 1105928 | tf_op jit(solution)/shard_map/ppermute | solution.py:325
  147.8 10.9 %collective-permute-start.38 = (f16[160,1152]{1,0:T(8,128)(2,1)S(1)}, f16[160,1152]{1,0:T(8,128)(2,1)S(1)}, u32[]{:S(2)}, u32[]{:S(2)}) collective-permute-start(f16[160,1152]{1,0:T(8,128)(2,1)S(1)} %get-tuple-element.102), channel_id=1, source_target_pairs={{0,12},{4,0},{8,4},{12,8},{1,13},{5,1},{9,5},{13,9},{2,14},{6,2},{... | collective-permute-start | bytes 1105928 | tf_op jit(solution)/shard_map/ppermute | solution.py:325
  (19 other events, 165.5 us)
